TPU v7x, 512 devices: a whole 4x4x16 slice. The times are simulated.
512 devices in a mesh: grp: 2 (over y_hi), seq: 32 (over z, core), dp: 8 (over x, y_lo).
Axes of the slice: x: 4, y: 4 (y_hi: 2, y_lo: 2; y = y_hi * 2 + y_lo), z: 16, core: 2. Of those that a mesh axis runs over, the one named last changes fastest.
Arguments:
- queries: bfloat16 [32, 2048, 2048], P(('grp', 'dp'), 'seq'), may hold values from -26 to 26
- key_states: bfloat16 [32, 2048, 2048], P(('grp', 'dp'), 'seq'), may hold values from -26 to 26
- value_states: bfloat16 [32, 2048, 2048], P(('grp', 'dp'), 'seq'), may hold values from -6 to 6
- projector: bfloat16 [2048, 1536], P('seq'), may hold values from -0.125 to 0.125
- teacher: bfloat16 [32, 2048, 1536], P(('grp', 'dp'), 'seq'), may hold values from -6 to 6
- enc_gain: float32 [1536], replicated, may hold values from 0.1 to 1.9
- enc_bias: float32 [1536], replicated, may hold values from -3 to 3
- valid_len: int32 [32], replicated, may hold values from 1 to 2048, 49152 in all
Outputs:
- grad_queries: bfloat16 [32, 2048, 2048], P(('grp', 'dp'), 'seq')
- grad_keys: bfloat16 [32, 2048, 2048], P(('grp', 'dp'), 'seq')
- grad_values: bfloat16 [32, 2048, 2048], P(('grp', 'dp'), 'seq')
Inputs may be any that keep to these rules, and one draw needn't show every extreme that they name: valid_len[b] counts the leading real tokens of image b; some image has all 2048.
All inputs are finite; a program needn't handle non-finite values.
Results may differ from a plain program's by a relative error of at most 0.025.
Values may be sent and summed in bfloat16 or wider, within the bound.
A program may use at most 128 MiB of HBM per device.

v0:
```python
import jax
import jax.numpy as jnp
from jax import lax
from jax.sharding import PartitionSpec as P

HD = 128


EPS = 1e-06
COEF = 2048.0


def from_partner(value, axis, apart):
    return lax.ppermute(value, axis, [(i, i ^ 1 << apart) for i in range(lax.axis_size(axis))])


def layer_norm(rows, gain, bias):
    data = rows.astype(jnp.float32)
    center = data - jnp.mean(data, axis=-1, keepdims=True)
    spread = jnp.mean(center * center, axis=-1, keepdims=True)
    return center * lax.rsqrt(spread + EPS) * gain + bias


def cosine_grad(aligned, target, keep):
    tgt = target.astype(jnp.float32)
    width = aligned.shape[-1]
    inner = jnp.mean(aligned * tgt, axis=-1, keepdims=True)
    own = jnp.mean(aligned * aligned, axis=-1, keepdims=True) + EPS
    other = jnp.mean(tgt * tgt, axis=-1, keepdims=True) + EPS
    inverse = lax.rsqrt(own * other)
    cosine = inner * inverse
    return -COEF / width * keep[..., None] * (tgt * inverse - cosine / own * aligned)


def to_heads(rows, ranks):
    count, seg, width = rows.shape
    heads = width // HD
    split = rows.reshape(count, seg, heads, HD).transpose(0, 2, 1, 3)
    return split.reshape(ranks, count * heads // ranks, seg, HD)


def from_heads(block, count):
    ranks, per, seg, depth = block.shape
    heads = ranks * per // count
    return (
        block.reshape(count, heads, seg, depth)
        .transpose(0, 2, 1, 3)
        .reshape(count, seg, heads * depth)
    )


def attend(qh, kh, key_keep, scale):
    scores = jnp.einsum("pid,pjd->pij", qh, kh, preferred_element_type=jnp.float32) * scale
    scores = jnp.where(key_keep[:, None, :], scores, -jnp.inf)
    top = jnp.max(scores, axis=-1, keepdims=True)
    expo = jnp.exp(scores - top)
    return expo / jnp.sum(expo, axis=-1, keepdims=True)


def to_blocks(data, blocks):
    per, total, depth = data.shape
    return data.reshape(per, blocks, total // blocks, depth).transpose(1, 0, 2, 3)


def from_blocks(data):
    blocks, per, rows, depth = data.shape
    return data.transpose(1, 0, 2, 3).reshape(per, blocks * rows, depth)


def shards(queries, key_states, value_states, projector, teacher, enc_gain, enc_bias, valid_len):
    ranks = lax.axis_size("seq")
    count, seg, width = queries.shape
    heads = width // HD
    per = count * heads // ranks
    total = seg * ranks
    rows_block = min(512, total)
    blocks = total // rows_block
    scale = HD ** (-0.5)
    moved = from_partner(teacher, "grp", 0)
    target = layer_norm(moved, enc_gain, enc_bias).astype(jnp.bfloat16)
    first_image = (lax.axis_index("grp") * lax.axis_size("dp") + lax.axis_index("dp")) * count
    local_len = lax.dynamic_slice_in_dim(valid_len, first_image, count)
    token_pos = lax.axis_index("seq") * seg + jnp.arange(seg, dtype=jnp.int32)
    token_keep = (token_pos[None, :] < local_len[:, None]).astype(jnp.float32)
    pair_ids = lax.axis_index("seq") * per + jnp.arange(per, dtype=jnp.int32)
    pair_image = pair_ids // heads
    match = pair_image[:, None] == jnp.arange(count, dtype=jnp.int32)[None, :]
    pair_len = jnp.sum(jnp.where(match, local_len[None, :], 0), axis=1)
    key_keep = jnp.arange(total, dtype=jnp.int32)[None, :] < pair_len[:, None]
    q_in, k_in, v_in = (
        lax.all_to_all(to_heads(queries, ranks), "seq", split_axis=0, concat_axis=2, tiled=True),
        lax.all_to_all(to_heads(key_states, ranks), "seq", split_axis=0, concat_axis=2, tiled=True),
        lax.all_to_all(
            to_heads(value_states, ranks), "seq", split_axis=0, concat_axis=2, tiled=True
        ),
    )
    qh = q_in.reshape(per, total, HD)
    kh = k_in.reshape(per, total, HD)
    vh = v_in.reshape(per, total, HD)
    q_blocks = to_blocks(qh, blocks)

    def forward_block(q_part):
        probs = attend(q_part, kh, key_keep, scale)
        probs_b = probs.astype(jnp.bfloat16)
        attended = jnp.einsum(
            "pij,pjd->pid", probs_b, vh, preferred_element_type=jnp.float32
        ).astype(jnp.bfloat16)
        return (attended, probs)

    att_blocks, kept_probs = lax.map(forward_block, q_blocks)
    attended = from_blocks(att_blocks)
    back = lax.all_to_all(
        attended.reshape(1, per, total, HD), "seq", split_axis=2, concat_axis=0, tiled=True
    )
    att_rows = from_heads(back, count).reshape(count * seg, width)
    whole = lax.all_gather(projector, "seq", axis=0, tiled=True)
    aligned = jnp.dot(att_rows, whole, preferred_element_type=jnp.float32)
    grad_aligned = cosine_grad(
        aligned, target.reshape(count * seg, -1), token_keep.reshape(count * seg)
    ).astype(jnp.bfloat16)
    grad_att = jnp.dot(grad_aligned, whole.T, preferred_element_type=jnp.float32)
    grad_att = grad_att.astype(jnp.bfloat16).reshape(count, seg, width)
    g_in = lax.all_to_all(to_heads(grad_att, ranks), "seq", split_axis=0, concat_axis=2, tiled=True)
    gh = g_in.reshape(per, total, HD)
    g_blocks = to_blocks(gh, blocks)

    def backward_block(carry, probs, q_part, g_part):
        acc_k, acc_v = carry
        probs_b = probs.astype(jnp.bfloat16)
        acc_v = acc_v + jnp.einsum(
            "pij,pid->pjd", probs_b, g_part, preferred_element_type=jnp.float32
        )
        grad_probs = jnp.einsum("pid,pjd->pij", g_part, vh, preferred_element_type=jnp.float32)
        delta = jnp.sum(probs * grad_probs, axis=-1, keepdims=True)
        grad_scores = (probs * (grad_probs - delta) * scale).astype(jnp.bfloat16)
        grad_q = jnp.einsum(
            "pij,pjd->pid", grad_scores, kh, preferred_element_type=jnp.float32
        ).astype(jnp.bfloat16)
        acc_k = acc_k + jnp.einsum(
            "pij,pid->pjd", grad_scores, q_part, preferred_element_type=jnp.float32
        )
        return ((acc_k, acc_v), grad_q)

    start = (jnp.zeros((per, total, HD), jnp.float32), jnp.zeros((per, total, HD), jnp.float32))

    def step_kept(carry, items):
        probs, q_part, g_part = items
        return backward_block(carry, probs, q_part, g_part)

    (acc_k, acc_v), gq_blocks = lax.scan(step_kept, start, (kept_probs, q_blocks, g_blocks))
    grad_q = from_blocks(gq_blocks)
    grad_k = acc_k.astype(jnp.bfloat16)
    grad_v = acc_v.astype(jnp.bfloat16)
    gq_back, gk_back, gv_back = (
        lax.all_to_all(
            grad_q.reshape(1, per, total, HD), "seq", split_axis=2, concat_axis=0, tiled=True
        ),
        lax.all_to_all(
            grad_k.reshape(1, per, total, HD), "seq", split_axis=2, concat_axis=0, tiled=True
        ),
        lax.all_to_all(
            grad_v.reshape(1, per, total, HD), "seq", split_axis=2, concat_axis=0, tiled=True
        ),
    )
    return (from_heads(gq_back, count), from_heads(gk_back, count), from_heads(gv_back, count))


def solution(mesh):
    return jax.shard_map(
        shards,
        mesh=mesh,
        in_specs=(
            P(("grp", "dp"), "seq", None),
            P(("grp", "dp"), "seq", None),
            P(("grp", "dp"), "seq", None),
            P("seq", None),
            P(("grp", "dp"), "seq", None),
            P(),
            P(),
            P(),
        ),
        out_specs=(
            P(("grp", "dp"), "seq", None),
            P(("grp", "dp"), "seq", None),
            P(("grp", "dp"), "seq", None),
        ),
        check_vma=False,
    )
```

profile of v0, /device:TPU:1, one launch (start us, length us, event | category | flops | bytes accessed | tf_op | source)
XLA Modules:
  0.0 476.0 jit_solution(947418801543016527)
XLA Ops:
  7.2 1.0 copy-done
  9.2 16.8 %all-to-all-start = ((bf16[32,1,64,128]{3,2,1,0:T(8,128)(2,1)}), bf16[32,1,64,128]{3,2,1,0:T(8,128)(2,1)S(1)}, u32[]{:S(2)}, u32[]{:S(2)}) async-start(bf16[32,1,64,128]{3,2,1,0:T(8,128)(2,1)} %bitcast.1), calls=%async_computation | async-start | bytes 1048576 | tf_op jit(solution)/shard_map/all_to_all | solution.py:91
  25.9 2.0 copy_bitcast_fusion.4
  27.9 31.5 %all-to-all-done = bf16[32,1,64,128]{3,2,1,0:T(8,128)(2,1)S(1)} async-done(((bf16[32,1,64,128]{3,2,1,0:T(8,128)(2,1)}), bf16[32,1,64,128]{3,2,1,0:T(8,128)(2,1)S(1)}, u32[]{:S(2)}, u32[]{:S(2)}) %all-to-all-start) | async-done | bytes 524320 | tf_op jit(solution)/shard_map/all_to_all | solution.py:91
  59.4 4.0 all-to-all-start.1
  64.4 32.6 %all-to-all-done.1 = bf16[32,1,64,128]{3,2,1,0:T(8,128)(2,1)S(1)} async-done(((bf16[32,1,64,128]{3,2,1,0:T(8,128)(2,1)}), bf16[32,1,64,128]{3,2,1,0:T(8,128)(2,1)S(1)}, u32[]{:S(2)}, u32[]{:S(2)}) %all-to-all-start.1) | async-done | bytes 524320 | tf_op jit(solution)/shard_map/all_to_all | solution.py:92
  97.0 5.0 %all-to-all-start.2 = ((bf16[32,1,64,128]{3,2,1,0:T(8,128)(2,1)}), bf16[32,1,64,128]{3,2,1,0:T(8,128)(2,1)}, u32[]{:S(2)}, u32[]{:S(2)}) async-start(bf16[32,1,64,128]{3,2,1,0:T(8,128)(2,1)} %bitcast.8), calls=%async_computation.2 | async-start | bytes 1048576 | tf_op jit(solution)/shard_map/all_to_all | solution.py:93
  103.5 31.9 %all-to-all-done.2 = bf16[32,1,64,128]{3,2,1,0:T(8,128)(2,1)} async-done(((bf16[32,1,64,128]{3,2,1,0:T(8,128)(2,1)}), bf16[32,1,64,128]{3,2,1,0:T(8,128)(2,1)}, u32[]{:S(2)}, u32[]{:S(2)}) %all-to-all-start.2) | async-done | bytes 524320 | tf_op jit(solution)/shard_map/all_to_all | solution.py:93
  135.4 29.8 %while.28 = (s32[]{:T(128)}, bf16[4,1,512,128]{3,2,1,0:T(8,128)(2,1)S(1)}, f32[4,1,512,2048]{3,2,1,0:T(8,128)}, bf16[4,1,512,128]{3,2,1,0:T(8,128)(2,1)S(1)}, bf...) while((s32[]{:T(128)}, ...), condition=%wide.region_4.5_spmd.clone, body=%wide.region_1.4_spmd.clone.sunk | while | flops 553714688 | bytes 22307424 | solution.py:110
  136.9 0.9 fusion.87
  137.8 2.9 bitcast_dynamic-update-slice_fusion.2
  140.7 2.2 fusion.88
  145.2 2.9 bitcast_dynamic-update-slice_fusion.2
  148.2 2.2 fusion.88
  151.8 0.9 fusion.87
  152.7 2.9 bitcast_dynamic-update-slice_fusion.2
  155.6 2.2 fusion.88
  159.3 0.9 fusion.87
  160.2 2.9 bitcast_dynamic-update-slice_fusion.2
  163.1 2.2 fusion.88
  165.3 8.1 %copy.108 = bf16[1,1,2048,128]{3,1,0,2:T(2,128)(2,1)S(1)} copy(bf16[1,1,2048,128]{3,2,1,0:T(8,128)(2,1)S(1)} %bitcast.221) | data formatting | bytes 1048576 | tf_op jit(solution)/shard_map/reshape;reshape;transpose | solution.py:113
  174.0 11.6 %reduce.11 = bf16[2048,128]{1,0:T(8,128)(2,1)S(1)} reduce(bf16[2048,1,1,128]{3,2,1,0:T(2,128)(2,1)S(1)} %bitcast.216, bf16[]{:T(256)} %broadcast.186), dimensions={1,2}, to_apply=%bitcast.173.reduce_sub_computation | reduce | bytes 1048578
  186.5 4.2 all-to-all-start.3
  190.8 4.8 %collective-permute-start = (bf16[2,64,1536]{2,1,0:T(8,128)(2,1)}, bf16[2,64,1536]{2,1,0:T(8,128)(2,1)S(1)}, u32[]{:S(2)}, u32[]{:S(2)}) collective-permute-start(bf16[2,64,1536]{2,1,0:T(8,128)(2,1)} %param.16), channel_id=1, source_target_pairs={{0,256},{256,0},{1,257},{257,1},{2,258},{258,2},{3,259},{259,3},{4... | collective-permute-start | bytes 1179656 | tf_op jit(solution)/shard_map/ppermute | solution.py:14
  195.8 8.9 %collective-permute-done = bf16[2,64,1536]{2,1,0:T(8,128)(2,1)S(1)} collective-permute-done((bf16[2,64,1536]{2,1,0:T(8,128)(2,1)}, bf16[2,64,1536]{2,1,0:T(8,128)(2,1)S(1)}, u32[]{:S(2)}, u32[]{:S(2)}) %collective-permute-start) | collective-permute-done | bytes 393248 | tf_op jit(solution)/shard_map/ppermute | solution.py:14
  205.6 18.7 %all-to-all-done.3 = bf16[32,2,4096]{2,1,0:T(2,128)(2,1)S(1)} async-done(((bf16[32,2,4096]{2,1,0:T(2,128)(2,1)}), bf16[32,2,4096]{2,1,0:T(2,128)(2,1)S(1)}, u32[]{:S(2)}, u32[]{:S(2)}) %all-to-all-start.3) | async-done | bytes 524320 | tf_op jit(solution)/shard_map/all_to_all | solution.py:112
  225.3 4.1 multiply_reduce_fusion
  229.9 2.1 fusion.44
  233.1 5.4 %all-to-all-start.4 = ((bf16[32,1,64,128]{3,2,1,0:T(8,128)(2,1)}), bf16[32,1,64,128]{3,2,1,0:T(8,128)(2,1)}, u32[]{:S(2)}, u32[]{:S(2)}) async-start(bf16[32,1,64,128]{3,2,1,0:T(8,128)(2,1)} %bitcast.17), calls=%async_computation.4 | async-start | bytes 1048576 | tf_op jit(solution)/shard_map/all_to_all | solution.py:123
  238.5 33.4 %all-to-all-done.4 = bf16[32,1,64,128]{3,2,1,0:T(8,128)(2,1)} async-done(((bf16[32,1,64,128]{3,2,1,0:T(8,128)(2,1)}), bf16[32,1,64,128]{3,2,1,0:T(8,128)(2,1)}, u32[]{:S(2)}, u32[]{:S(2)}) %all-to-all-start.4) | async-done | bytes 524320 | tf_op jit(solution)/shard_map/all_to_all | solution.py:123
  272.8 58.1 %while.29 = (s32[]{:T(128)}, f32[1,2048,128]{2,1,0:T(8,128)}, f32[1,2048,128]{2,1,0:T(8,128)}, bf16[4,1,512,128]{3,2,1,0:T(8,128)(2,1)}, f32[4,1,512,2048]{3,2,1...) while((s32[]{:T(128)}, f32[1,2048,128]{2,1,0:T(8,128)}, ...), condition=%wide.region_12.13_spmd.clone, body=%wide.region_10.12_spmd.clone.sunk | while | flops 1081146880 | bytes 30940280 | solution.py:150
  272.8 3.2 fusion.95
  276.0 2.8 fusion.96
  278.8 2.6 fusion.97
  281.4 1.4 fusion.99
  282.8 4.0 fusion.98
  286.8 3.2 fusion.95
  289.9 2.8 fusion.96
  292.7 3.0 fusion.97
  295.8 1.4 fusion.99
  297.2 4.3 fusion.98
  301.5 3.2 fusion.95
  304.6 2.8 fusion.96
  307.5 3.0 fusion.97
  310.5 1.4 fusion.99
  311.9 4.3 fusion.98
  316.2 3.2 fusion.95
  319.3 2.8 fusion.96
  322.2 3.0 fusion.97
  325.2 1.4 fusion.99
  326.6 4.3 fusion.98
  330.9 1.7 convert_bitcast_fusion
  332.5 8.1 %copy.105 = bf16[1,1,2048,128]{3,1,0,2:T(2,128)(2,1)S(1)} copy(bf16[1,1,2048,128]{3,2,1,0:T(8,128)(2,1)S(1)} %get-tuple-element.251) | data formatting | bytes 1048576 | tf_op jit(solution)/shard_map/reshape | solution.py:162
  340.7 11.5 %reduce.14 = bf16[2048,128]{1,0:T(8,128)(2,1)S(1)} reduce(bf16[2048,1,1,128]{3,2,1,0:T(2,128)(2,1)S(1)} %bitcast.218, bf16[]{:T(256)} %broadcast.186), dimensions={1,2}, to_apply=%bitcast.170.reduce_sub_computation | reduce | bytes 1048578
  353.1 4.9 %all-to-all-start.7 = ((bf16[32,2,4096]{2,1,0:T(2,128)(2,1)}), bf16[32,2,4096]{2,1,0:T(2,128)(2,1)S(1)}, u32[]{:S(2)}, u32[]{:S(2)}) async-start(bf16[32,2,4096]{2,1,0:T(2,128)(2,1)} %reshape.306), calls=%async_computation.7 | async-start | bytes 1048576 | tf_op jit(solution)/shard_map/all_to_all | solution.py:161
  358.0 8.1 %copy.106 = bf16[1,1,2048,128]{3,1,0,2:T(2,128)(2,1)S(1)} copy(bf16[1,1,2048,128]{3,2,1,0:T(8,128)(2,1)S(1)} %get-tuple-element.252) | data formatting | bytes 1048576 | tf_op jit(solution)/shard_map/reshape | solution.py:159
  366.1 11.4 %reduce.13 = bf16[2048,128]{1,0:T(8,128)(2,1)S(1)} reduce(bf16[2048,1,1,128]{3,2,1,0:T(2,128)(2,1)S(1)} %bitcast.219, bf16[]{:T(256)} %broadcast.186), dimensions={1,2}, to_apply=%bitcast.171.reduce_sub_computation | reduce | bytes 1048578
  378.5 12.9 %all-to-all-done.7 = bf16[32,2,4096]{2,1,0:T(2,128)(2,1)S(1)} async-done(((bf16[32,2,4096]{2,1,0:T(2,128)(2,1)}), bf16[32,2,4096]{2,1,0:T(2,128)(2,1)S(1)}, u32[]{:S(2)}, u32[]{:S(2)}) %all-to-all-start.7) | async-done | bytes 524320 | tf_op jit(solution)/shard_map/all_to_all | solution.py:161
  391.4 4.6 all-to-all-start.6
  396.1 8.1 %copy.107 = bf16[1,1,2048,128]{3,1,0,2:T(2,128)(2,1)S(1)} copy(bf16[1,1,2048,128]{3,2,1,0:T(8,128)(2,1)S(1)} %bitcast.220) | data formatting | bytes 1048576 | tf_op jit(solution)/shard_map/reshape;reshape;transpose | solution.py:156
  404.2 11.4 %reduce.12 = bf16[2048,128]{1,0:T(8,128)(2,1)S(1)} reduce(bf16[2048,1,1,128]{3,2,1,0:T(2,128)(2,1)S(1)} %bitcast.217, bf16[]{:T(256)} %broadcast.186), dimensions={1,2}, to_apply=%bitcast.172.reduce_sub_computation | reduce | bytes 1048578
  416.6 12.9 %all-to-all-done.6 = bf16[32,2,4096]{2,1,0:T(2,128)(2,1)S(1)} async-done(((bf16[32,2,4096]{2,1,0:T(2,128)(2,1)}), bf16[32,2,4096]{2,1,0:T(2,128)(2,1)S(1)}, u32[]{:S(2)}, u32[]{:S(2)}) %all-to-all-start.6) | async-done | bytes 524320 | tf_op jit(solution)/shard_map/all_to_all | solution.py:158
  429.5 4.3 all-to-all-start.5
  436.9 30.4 %all-to-all-done.5 = bf16[32,2,4096]{2,1,0:T(2,128)(2,1)S(1)} async-done(((bf16[32,2,4096]{2,1,0:T(2,128)(2,1)}), bf16[32,2,4096]{2,1,0:T(2,128)(2,1)S(1)}, u32[]{:S(2)}, u32[]{:S(2)}) %all-to-all-start.5) | async-done | bytes 524320 | tf_op jit(solution)/shard_map/all_to_all | solution.py:155
  (66 shorter events, 23.2 us)
Async XLA Ops:
  7.2 1.0 copy-start
  7.2 56.3 %copy-start.4 = (bf16[2,64,2048]{2,1,0:T(8,128)(2,1)S(1)}, bf16[2,64,2048]{2,1,0:T(8,128)(2,1)}, u32[]{:S(2)}) copy-start(bf16[2,64,2048]{2,1,0:T(8,128)(2,1)} %param.14) | copy-start | bytes 1572868
  7.2 95.6 %copy-start.7 = (s32[32]{0:T(128)S(1)}, s32[32]{0:T(128)}, u32[]{:S(2)}) copy-start(s32[32]{0:T(128)} %param.19) | copy-start | bytes 388
  9.2 50.3 %all-to-all-start = ((bf16[32,1,64,128]{3,2,1,0:T(8,128)(2,1)}), bf16[32,1,64,128]{3,2,1,0:T(8,128)(2,1)S(1)}, u32[]{:S(2)}, u32[]{:S(2)}) async-start(bf16[32,1,64,128]{3,2,1,0:T(8,128)(2,1)} %bitcast.1), calls=%async_computation | async-start | bytes 1048576 | tf_op jit(solution)/shard_map/all_to_all | solution.py:91
  59.4 37.6 %all-to-all-start.1 = ((bf16[32,1,64,128]{3,2,1,0:T(8,128)(2,1)}), bf16[32,1,64,128]{3,2,1,0:T(8,128)(2,1)S(1)}, u32[]{:S(2)}, u32[]{:S(2)}) async-start(bf16[32,1,64,128]{3,2,1,0:T(8,128)(2,1)} %bitcast.5), calls=%async_computation.1 | async-start | bytes 1048576 | tf_op jit(solution)/shard_map/all_to_all | solution.py:92
  97.0 38.4 %all-to-all-start.2 = ((bf16[32,1,64,128]{3,2,1,0:T(8,128)(2,1)}), bf16[32,1,64,128]{3,2,1,0:T(8,128)(2,1)}, u32[]{:S(2)}, u32[]{:S(2)}) async-start(bf16[32,1,64,128]{3,2,1,0:T(8,128)(2,1)} %bitcast.8), calls=%async_computation.2 | async-start | bytes 1048576 | tf_op jit(solution)/shard_map/all_to_all | solution.py:93
  102.0 123.3 %all-gather.2.cloned.1.call-start = ((), (), s32[]{:S(2)}) async-start(), calls=%async_computation.8 | async-start | bytes 6488064 | tf_op jit(solution)/shard_map/all_gather | solution.py:116
  165.3 21.2 %copy-start.2 = (bf16[4,1,512,128]{3,2,1,0:T(8,128)(2,1)}, bf16[4,1,512,128]{3,2,1,0:T(8,128)(2,1)S(1)}, u32[]{:S(2)}) copy-start(bf16[4,1,512,128]{3,2,1,0:T(8,128)(2,1)S(1)} %get-tuple-element.422) | copy-start | bytes 1572868
  165.3 39.8 %copy-start.5 = (f32[1536]{0:T(1024)S(1)}, f32[1536]{0:T(1024)}, u32[]{:S(2)}) copy-start(f32[1536]{0:T(1024)} %param.18) | copy-start | bytes 18436
  165.3 39.8 %copy-start.6 = (f32[1536]{0:T(1024)S(1)}, f32[1536]{0:T(1024)}, u32[]{:S(2)}) copy-start(f32[1536]{0:T(1024)} %param.17) | copy-start | bytes 18436
  186.5 37.8 %all-to-all-start.3 = ((bf16[32,2,4096]{2,1,0:T(2,128)(2,1)}), bf16[32,2,4096]{2,1,0:T(2,128)(2,1)S(1)}, u32[]{:S(2)}, u32[]{:S(2)}) async-start(bf16[32,2,4096]{2,1,0:T(2,128)(2,1)} %reshape.300), calls=%async_computation.3 | async-start | bytes 1048576 | tf_op jit(solution)/shard_map/all_to_all | solution.py:112
  190.8 14.0 %collective-permute-start = (bf16[2,64,1536]{2,1,0:T(8,128)(2,1)}, bf16[2,64,1536]{2,1,0:T(8,128)(2,1)S(1)}, u32[]{:S(2)}, u32[]{:S(2)}) collective-permute-start(bf16[2,64,1536]{2,1,0:T(8,128)(2,1)} %param.16), channel_id=1, source_target_pairs={{0,256},{256,0},{1,257},{257,1},{2,258},{258,2},{3,259},{259,3},{4... | collective-permute-start | bytes 1179656 | tf_op jit(solution)/shard_map/ppermute | solution.py:14
  225.3 4.6 copy-start.1
  233.1 38.8 %all-to-all-start.4 = ((bf16[32,1,64,128]{3,2,1,0:T(8,128)(2,1)}), bf16[32,1,64,128]{3,2,1,0:T(8,128)(2,1)}, u32[]{:S(2)}, u32[]{:S(2)}) async-start(bf16[32,1,64,128]{3,2,1,0:T(8,128)(2,1)} %bitcast.17), calls=%async_computation.4 | async-start | bytes 1048576 | tf_op jit(solution)/shard_map/all_to_all | solution.py:123
  340.7 55.4 %copy-start.3 = (bf16[4,1,512,128]{3,2,1,0:T(8,128)(2,1)S(1)}, bf16[4,1,512,128]{3,2,1,0:T(8,128)(2,1)}, u32[]{:S(2)}) copy-start(bf16[4,1,512,128]{3,2,1,0:T(8,128)(2,1)} %get-tuple-element.92) | copy-start | bytes 1572868
  353.1 38.3 %all-to-all-start.7 = ((bf16[32,2,4096]{2,1,0:T(2,128)(2,1)}), bf16[32,2,4096]{2,1,0:T(2,128)(2,1)S(1)}, u32[]{:S(2)}, u32[]{:S(2)}) async-start(bf16[32,2,4096]{2,1,0:T(2,128)(2,1)} %reshape.306), calls=%async_computation.7 | async-start | bytes 1048576 | tf_op jit(solution)/shard_map/all_to_all | solution.py:161
  391.4 38.1 %all-to-all-start.6 = ((bf16[32,2,4096]{2,1,0:T(2,128)(2,1)}), bf16[32,2,4096]{2,1,0:T(2,128)(2,1)S(1)}, u32[]{:S(2)}, u32[]{:S(2)}) async-start(bf16[32,2,4096]{2,1,0:T(2,128)(2,1)} %reshape.304), calls=%async_computation.6 | async-start | bytes 1048576 | tf_op jit(solution)/shard_map/all_to_all | solution.py:158
  429.5 37.9 %all-to-all-start.5 = ((bf16[32,2,4096]{2,1,0:T(2,128)(2,1)}), bf16[32,2,4096]{2,1,0:T(2,128)(2,1)S(1)}, u32[]{:S(2)}, u32[]{:S(2)}) async-start(bf16[32,2,4096]{2,1,0:T(2,128)(2,1)} %reshape.302), calls=%async_computation.5 | async-start | bytes 1048576 | tf_op jit(solution)/shard_map/all_to_all | solution.py:155
Sparse Core Ops, SparseCore 0:
  105.0 80.3 all-gather.1
where the time goes:
time: 485 us; the launch traced here: 476 us
  waiting for transfers between devices  214 us (44%)
  other arithmetic  78.5 us (16%)
  matrix products  65.1 us (13%)
  starting transfers between devices  54.1 us (11%)
  local copies, waits for them, and re-layouts  49.5 us (10%)
  between operations  14.6 us (3%)
    unnamed x6, other arithmetic  46 us
    all_to_all x1, waiting for transfers between devices, shards(): lax.all_to_all(to_heads(grad_att, ranks), 'seq', split_axis=0, concat_axi...  33.4 us
    all_to_all x1, waiting for transfers between devices, shards(): lax.all_to_all(to_heads(key_states, ranks), 'seq', split_axis=0, concat_a...  32.6 us
    all_to_all x1, waiting for transfers between devices, shards(): lax.all_to_all(to_heads(value_states, ranks), 'seq', split_axis=0, concat...  31.9 us
    all_to_all x1, waiting for transfers between devices, shards(): lax.all_to_all(to_heads(queries, ranks), 'seq', split_axis=0, concat_axis...  31.5 us
    all_to_all x1, waiting for transfers between devices, shards(): lax.all_to_all(grad_q.reshape(1, per, total, HD), 'seq', split_axis=2, co...  30.4 us
    all_to_all x1, waiting for transfers between devices, shards(): lax.all_to_all(attended.reshape(1, per, total, HD), 'seq', split_axis=2,...  18.7 us
    dot_general x4, matrix products, backward_block(): jnp.einsum('pij,pid->pjd', probs_b, g_part, preferred_element_type=jnp.fl...  16.9 us
  transfers between devices with their start and end apart: 10, of which 9 were waited for; matrix products, arithmetic and copies ran while one was open for 21% of the time, Pallas kernels for 0%

commit v1 on v0

v1 whole, which is shorter than its diff:
```python
import functools

import jax
import jax.numpy as jnp
from jax import lax
from jax.experimental import pallas as pl
from jax.experimental.pallas import tpu as pltpu
from jax.sharding import PartitionSpec as P

HD = 128
SEG = 64
TOK = 2 * SEG
EPS = 1e-06
COEF = 2048.0
LOG2E = 1.4426950408889634
MESH = pl.DeviceIdType.MESH
BF = jnp.bfloat16
F32 = jnp.float32
NT = (((1,), (1,)), ((), ()))


def al(value, step):
    return pl.multiple_of(value, step)


def kernel(
    nz, nr, ndp, bq,
    q_ref, k_ref, v_ref, w_ref, t_ref, gain_ref, bias_ref, kb_ref, keep_ref,
    oq_ref, ok_ref, ov_ref,
    qh, kh, va, wf, tea, att_h, rows, gsend, gh, gq_h, gk_h, gv_h,
    expo, att_f, linv, aligned, gal, acc_k, acc_v,
    in_send, in_recv, w_send, w_recv, t_send, t_recv, mid_send, mid_recv, out_send, out_recv,
):
    ns = 2 * nz
    total = ns * SEG
    enc = t_ref.shape[-1]
    cq = nr // 4
    cw = enc // cq
    nb = total // bq
    per = bq // TOK
    scale = HD ** (-0.5)

    me = lax.axis_index("seq")
    grp = lax.axis_index("grp")
    ring = grp * ndp + lax.axis_index("dp")
    z = me // 2
    c = lax.rem(me, 2)

    def on_ring(s):
        return {"seq": s}

    def in_plane(r):
        return {"grp": r // ndp, "dp": lax.rem(r, ndp)}

    def across(s):
        return {"grp": 1 - grp, "seq": s}

    barrier = pltpu.get_barrier_semaphore()

    def greet(device):
        pl.semaphore_signal(barrier, 1, device_id=device, device_id_type=MESH)

    @pl.loop(1, ns)
    def _(step):
        greet(on_ring(lax.rem(me + step, ns)))

    @pl.loop(1, nr)
    def _(step):
        greet(in_plane(lax.rem(ring + step, nr)))

    greet(across(2 * z + 1 - c))
    pl.semaphore_wait(barrier, ns - 1 + nr - 1 + 1)

    def remote(src, dst, ssem, rsem, device):
        return pltpu.make_async_remote_copy(
            src_ref=src, dst_ref=dst, send_sem=ssem, recv_sem=rsem, device_id=device, device_id_type=MESH
        )

    def waiting(view, sem):
        pltpu.make_async_copy(view, view, sem).wait()

    for image in range(2):
        remote(
            t_ref.at[image], tea.at[c], t_send, t_recv, across(2 * z + image)
        ).start()

    band = ring // cq
    wcols = pl.ds(al(lax.rem(ring, cq) * cw, 128), cw)
    own_w = w_ref.at[band, :, wcols]

    @pl.loop(1, nz)
    def _(step):
        there = lax.rem(z + step, nz)
        remote(
            own_w, wf.at[z, c, band, :, wcols], w_send.at[0], w_recv.at[0], on_ring(2 * there + c)
        ).start()

    pltpu.make_async_copy(own_w, wf.at[z, c, band, :, wcols], w_recv.at[0]).start()

    mine = pl.ds(al(me * SEG, SEG), SEG)
    sources = (k_ref, q_ref, v_ref)
    places = (kh.at[mine], qh.at[mine], va.at[mine, pl.ds(0, HD)])

    def send_inputs(image):
        for a in range(3):
            @pl.loop(1, nz)
            def _(step):
                there = lax.rem(z + step, nz)
                cols = pl.ds(al(there * HD, HD), HD)
                remote(
                    sources[a].at[image, :, cols], places[a], in_send.at[a], in_recv.at[a],
                    on_ring(2 * there + image),
                ).start()

            own = sources[a].at[image, :, pl.ds(al(z * HD, HD), HD)]

            @pl.when(c == image)
            def _():
                pltpu.make_async_copy(own, places[a], in_recv.at[a]).start()

            @pl.when(c != image)
            def _():
                remote(
                    own, places[a], in_send.at[a], in_recv.at[a], on_ring(2 * z + image)
                ).start()

    send_inputs(0)

    part_w = wf.at[:, c, band, :, wcols]
    waiting(part_w, w_recv.at[0])

    @pl.loop(1, nr)
    def _(step):
        remote(
            part_w, part_w, w_send.at[1], w_recv.at[1], in_plane(lax.rem(ring + step, nr))
        ).start()

    send_inputs(1)

    va[:, HD:] = jnp.ones((total, HD), BF)
    acc_k[...] = jnp.zeros_like(acc_k)
    acc_v[...] = jnp.zeros_like(acc_v)

    def swap_w():
        waiting(wf.at[pl.ds(0, nr - 1), c], w_recv.at[1])
        half = wf.at[:, c]
        remote(half, half, w_send.at[2], w_recv.at[2], on_ring(2 * z + 1 - c)).start()

    @pl.when(c == 1)
    def _():
        swap_w()

    waiting(tea, t_recv)
    for seg in range(2):
        data = tea[seg].astype(F32)
        center = data - jnp.mean(data, axis=-1, keepdims=True)
        spread = jnp.mean(center * center, axis=-1, keepdims=True)
        tea[seg] = (center * lax.rsqrt(spread + EPS) * gain_ref[...] + bias_ref[...]).astype(BF)

    waiting(kh, in_recv.at[0])
    waiting(qh, in_recv.at[1])
    waiting(va.at[:, pl.ds(0, HD)], in_recv.at[2])

    first = z // per

    @pl.loop(0, nb)
    def _(step):
        block = lax.rem(first + step, nb)
        span = pl.ds(al(block * bq, bq), bq)
        scores = lax.dot_general(qh[span], kh[...], NT, preferred_element_type=F32)
        scores = scores * (scale * LOG2E) + kb_ref[...]
        top = jnp.max(scores, axis=-1, keepdims=True)
        raised = jnp.exp2(scores - top).astype(BF)
        expo[span] = raised
        both = jnp.dot(raised, va[...], preferred_element_type=F32)
        inverse = 1.0 / both[:, HD:]
        attended = both[:, :HD] * inverse
        linv[span] = inverse
        att_f[span] = attended
        att_h[span] = attended.astype(BF)
        for part in range(per):
            there = block * per + part
            src = att_h.at[pl.ds(al(there * TOK, TOK), TOK)]
            dst = rows.at[:, pl.ds(al(z * HD, HD), HD)]

            @pl.when(there == z)
            def _():
                pltpu.make_async_copy(src, dst, mid_recv.at[0]).start()

            @pl.when(there != z)
            def _():
                remote(src, dst, mid_send.at[0], mid_recv.at[0], on_ring(2 * there + c)).start()

    @pl.when(c == 0)
    def _():
        swap_w()

    waiting(wf.at[:, 1 - c], w_recv.at[2])
    waiting(rows, mid_recv.at[0])

    pieces = enc // 384
    inner = jnp.zeros((TOK, 1), F32)
    own = jnp.zeros((TOK, 1), F32)
    other = jnp.zeros((TOK, 1), F32)
    for piece in range(pieces):
        cols = slice(piece * 384, (piece + 1) * 384)
        weights = wf[:, :, :, :, cols].reshape(nz * HD, 384)
        out = jnp.dot(rows[...], weights, preferred_element_type=F32)
        aligned[:, cols] = out
        tgt = tea[:, :, cols].reshape(TOK, 384).astype(F32)
        inner += jnp.sum(out * tgt, axis=-1, keepdims=True)
        own += jnp.sum(out * out, axis=-1, keepdims=True)
        other += jnp.sum(tgt * tgt, axis=-1, keepdims=True)
    inner = inner / enc
    own = own / enc + EPS
    other = other / enc + EPS
    inverse = lax.rsqrt(own * other)
    cosine = inner * inverse
    kept = keep_ref[...] * (-COEF / enc)
    left = kept * inverse
    right = kept * (cosine / own)
    for piece in range(pieces):
        cols = slice(piece * 384, (piece + 1) * 384)
        tgt = tea[:, :, cols].reshape(TOK, 384).astype(F32)
        gal[:, cols] = (tgt * left - right * aligned[:, cols]).astype(BF)

    @pl.loop(0, nz // 2)
    def _(step):
        pair = lax.rem(z // 2 + step, nz // 2)
        weights = wf[pl.ds(pair * 2, 2)].reshape(2 * HD, enc)
        back = lax.dot_general(gal[...], weights, NT, preferred_element_type=F32).astype(BF)
        for part in range(2):
            there = pair * 2 + part
            gsend[there] = back[:, part * HD:(part + 1) * HD]
            src = gsend.at[there]
            dst = gh.at[pl.ds(al(z * TOK, TOK), TOK)]

            @pl.when(there == z)
            def _():
                pltpu.make_async_copy(src, dst, mid_recv.at[1]).start()

            @pl.when(there != z)
            def _():
                remote(src, dst, mid_send.at[1], mid_recv.at[1], on_ring(2 * there + c)).start()

    waiting(gh, mid_recv.at[1])

    my_cols = pl.ds(al(z * HD, HD), HD)

    def send_out(src_ref, out_ref, a, s):
        src = src_ref.at[pl.ds(al(s * SEG, SEG), SEG)]
        dst = out_ref.at[c, :, my_cols]

        @pl.when(s == me)
        def _():
            pltpu.make_async_copy(src, dst, out_recv.at[a]).start()

        @pl.when(s != me)
        def _():
            remote(src, dst, out_send.at[a], out_recv.at[a], on_ring(s)).start()

    segs = bq // SEG

    @pl.loop(0, nb)
    def _(step):
        block = lax.rem(first + step, nb)
        span = pl.ds(al(block * bq, bq), bq)
        grad = gh[span].astype(F32) * linv[span]
        grad_b = grad.astype(BF)
        delta = jnp.sum(grad_b.astype(F32) * att_f[span], axis=-1, keepdims=True)
        raised = expo[span]
        grad_p = lax.dot_general(grad_b, va[:, :HD], NT, preferred_element_type=F32)
        grad_s = (raised.astype(F32) * (grad_p - delta)).astype(BF)
        acc_v[...] += jnp.dot(grad.T.astype(BF), raised, preferred_element_type=F32)
        acc_k[...] += jnp.dot(qh[span].astype(F32).T.astype(BF), grad_s, preferred_element_type=F32)
        grad_q = jnp.dot(grad_s, kh[...], preferred_element_type=F32)
        gq_h[span] = (grad_q * scale).astype(BF)
        for part in range(segs):
            send_out(gq_h, oq_ref, 0, block * segs + part)

    gv_h[...] = acc_v[...].T.astype(BF)

    @pl.loop(0, ns)
    def _(step):
        send_out(gv_h, ov_ref, 2, lax.rem(me + step, ns))

    gk_h[...] = (acc_k[...] * scale).T.astype(BF)

    @pl.loop(0, ns)
    def _(step):
        send_out(gk_h, ok_ref, 1, lax.rem(me + step, ns))

    waiting(tea, t_send)
    waiting(wf.at[pl.ds(0, nz - 1), c, band, :, wcols], w_send.at[0])
    waiting(wf.at[pl.ds(0, nr - 1), c], w_send.at[1])
    waiting(wf.at[:, c], w_send.at[2])
    most = pl.ds(0, total - SEG)
    for a, buf in enumerate((kh.at[most], qh.at[most], va.at[most, pl.ds(0, HD)])):
        waiting(buf, in_send.at[a])
    waiting(att_h.at[pl.ds(0, total - TOK)], mid_send.at[0])
    waiting(gsend.at[pl.ds(0, nz - 1)], mid_send.at[1])
    for a, buf in enumerate((gq_h, gk_h, gv_h)):
        waiting(buf.at[most], out_send.at[a])
    for a, buf in enumerate((oq_ref, ok_ref, ov_ref)):
        waiting(buf, out_recv.at[a])


def shards(queries, key_states, value_states, projector, teacher, enc_gain, enc_bias, valid_len):
    ns = lax.axis_size("seq")
    nz = ns // 2
    ndp = lax.axis_size("dp")
    nr = ndp * lax.axis_size("grp")
    count, seg, width = queries.shape
    enc = teacher.shape[-1]
    total = ns * seg
    bq = min(256, total // 2)
    me = lax.axis_index("seq")
    image = (lax.axis_index("grp") * ndp + lax.axis_index("dp")) * count + lax.rem(me, 2)
    length = lax.dynamic_slice_in_dim(valid_len, image, 1)
    key_bias = jnp.where(lax.iota(jnp.int32, total) < length, 0.0, -1e30).astype(F32)[None, :]
    token = (me // 2) * TOK + lax.iota(jnp.int32, TOK)
    keep = (token < length).astype(F32)[:, None]
    vm = pl.BlockSpec(memory_space=pltpu.VMEM)
    hbm = pl.BlockSpec(memory_space=pl.ANY)
    dma = pltpu.SemaphoreType.DMA
    head = pltpu.VMEM((total, HD), BF)
    head_f = pltpu.VMEM((total, HD), F32)
    out = jax.ShapeDtypeStruct(queries.shape, BF)
    return pl.pallas_call(
        functools.partial(kernel, nz, nr, ndp, bq),
        out_shape=[out, out, out],
        in_specs=[hbm, hbm, hbm, hbm, hbm, vm, vm, vm, vm],
        out_specs=[hbm, hbm, hbm],
        scratch_shapes=[
            head,
            head,
            pltpu.VMEM((total, 2 * HD), BF),
            pltpu.VMEM((nz, 2, 4, seg // 4, enc), BF),
            pltpu.VMEM((2, seg, enc), BF),
            head,
            pltpu.VMEM((TOK, width), BF),
            pltpu.VMEM((nz, TOK, HD), BF),
            head,
            head,
            head,
            head,
            pltpu.VMEM((total, total), BF),
            head_f,
            head_f,
            pltpu.VMEM((TOK, enc), F32),
            pltpu.VMEM((TOK, enc), BF),
            pltpu.VMEM((HD, total), F32),
            pltpu.VMEM((HD, total), F32),
            dma((3,)),
            dma((3,)),
            dma((3,)),
            dma((3,)),
            dma,
            dma,
            dma((2,)),
            dma((2,)),
            dma((3,)),
            dma((3,)),
        ],
        compiler_params=pltpu.CompilerParams(
            collective_id=0, has_side_effects=True, vmem_limit_bytes=58 << 20
        ),
    )(
        queries,
        key_states,
        value_states,
        projector.reshape(4, seg // 4, enc),
        teacher,
        enc_gain[None, :],
        enc_bias[None, :],
        key_bias,
        keep,
    )


def solution(mesh):
    rows = P(("grp", "dp"), "seq", None)
    return jax.shard_map(
        shards,
        mesh=mesh,
        in_specs=(rows, rows, rows, P("seq", None), rows, P(), P(), P()),
        out_specs=(rows, rows, rows),
        check_vma=False,
    )
```

time: 485 us -> 223 us (0.46)
  the two profiles are of different devices: /device:TPU:1 before, /device:TPU:31 now
where the time goes in v1:
time: 223 us
  Pallas kernels  213 us (96%)
  local copies, waits for them, and re-layouts  6.5 us (3%)
  other arithmetic  2.36 us (1%)
    pallas_call x1, Pallas kernels, shards(): pl.pallas_call(functools.partial(kernel, nz, nr, ndp, bq), out_shape=[out...  213 us
    unnamed x13, local copies, waits for them, and re-layouts  4.72 us

profile of v1, /device:TPU:31, one launch (start us, length us, event | category | flops | bytes accessed | tf_op | source)
XLA Modules:
  0.0 222.9 jit_solution(1968488920356764967)
XLA Ops:
  0.6 0.0 copy-start.2
  0.7 0.0 copy-start.4
  0.7 0.6 copy-done.4
  1.3 0.6 dynamic_slice.3
  1.9 0.0 copy-start.3
  1.9 0.0 copy-done.2
  1.9 0.6 broadcast_in_dim.16.gain_ref
  2.5 0.1 copy-done.3
  2.6 0.6 broadcast_in_dim.17.bias_ref
  3.2 1.2 compare_select_fusion.kb_ref
  4.4 1.2 fusion.keep_ref
  5.6 213.4 %shard_map.103 = (bf16[2,64,2048]{2,1,0:T(8,128)(2,1)}, bf16[2,64,2048]{2,1,0:T(8,128)(2,1)}, bf16[2,64,2048]{2,1,0:T(8,128)(2,1)}) custom-call(bf16[2,64,2048]{2,1,0:T(8,128)(2,1)} %q_ref.1, bf16[2,64,2048]{2,1,0:T(8,128)(2,1)} %k_ref.1, bf16[2,64,2048]{2,1,0:T(8,128)(2,1)} %v_ref.1, bf16[4,16,1536]{2,1,0:T(8,128)(2,1)} %bitcast.2, ...), custom_call_target="tpu_custom_call" | custom-call | tf_op jit(solution)/shard_map/pallas_call | solution.py:329
  219.0 0.0 copy-start.1
  219.0 1.9 copy.15
  220.9 0.0 copy-done.1
  220.9 0.0 copy-start
  220.9 0.8 copy.16
  221.7 0.4 copy-done
  222.1 0.8 copy.17
Async XLA Ops:
  0.6 1.3 copy-start.2
  0.7 0.7 copy-start.4
  1.9 0.7 copy-start.3
  219.0 2.0 copy-start.1
  220.9 1.2 copy-start

commit v2 on v1

--- a/solution.py
+++ b/solution.py
@@ -25,11 +25,11 @@
 
 def kernel(
     nz, nr, ndp, bq,
-    q_ref, k_ref, v_ref, w_ref, t_ref, gain_ref, bias_ref, kb_ref, keep_ref,
+    q_ref, k_ref, v_ref, w_ref, t_ref, gain_ref, bias_ref, len_ref,
     oq_ref, ok_ref, ov_ref,
-    qh, kh, va, wf, tea, att_h, rows, gsend, gh, gq_h, gk_h, gv_h,
+    stage, t_stage, kb_ref, qh, kh, va, wf, tea, att_h, rows, gsend, gh, gq_h, gk_h, gv_h,
     expo, att_f, linv, aligned, gal, acc_k, acc_v,
-    in_send, in_recv, w_send, w_recv, t_send, t_recv, mid_send, mid_recv, out_send, out_recv,
+    st_send, st_recv, in_send, in_recv, w_send, w_recv, t_send, t_recv, mid_send, mid_recv, out_send, out_recv,
 ):
     ns = 2 * nz
     total = ns * SEG
@@ -38,11 +38,12 @@
     cw = enc // cq
     nb = total // bq
     per = bq // TOK
+    tq = min(4, nr // 2)
+    tc = nr // (2 * tq)
     scale = HD ** (-0.5)
 
     me = lax.axis_index("seq")
-    grp = lax.axis_index("grp")
-    ring = grp * ndp + lax.axis_index("dp")
+    ring = lax.axis_index("grp") * ndp + lax.axis_index("dp")
     z = me // 2
     c = lax.rem(me, 2)
 
@@ -52,8 +53,8 @@
     def in_plane(r):
         return {"grp": r // ndp, "dp": lax.rem(r, ndp)}
 
-    def across(s):
-        return {"grp": 1 - grp, "seq": s}
+    def at(r, s):
+        return {"grp": r // ndp, "dp": lax.rem(r, ndp), "seq": s}
 
     barrier = pltpu.get_barrier_semaphore()
 
@@ -68,8 +69,21 @@
     def _(step):
         greet(in_plane(lax.rem(ring + step, nr)))
 
-    greet(across(2 * z + 1 - c))
-    pl.semaphore_wait(barrier, ns - 1 + nr - 1 + 1)
+    @pl.loop(0, nr)
+    def _(step):
+        head = lax.rem(ring + step, nr)
+        for core in range(2):
+            @pl.when((head != ring) & (2 * ring + core != me))
+            def _():
+                greet(at(head, 2 * ring + core))
+
+    @pl.when(ring == z)
+    def _():
+        pl.semaphore_wait(barrier, ns - 1 + nr - 1)
+
+    @pl.when(ring != z)
+    def _():
+        pl.semaphore_wait(barrier, 2 * (ns - 1) + nr - 1)
 
     def remote(src, dst, ssem, rsem, device):
         return pltpu.make_async_remote_copy(
@@ -79,11 +93,6 @@
     def waiting(view, sem):
         pltpu.make_async_copy(view, view, sem).wait()
 
-    for image in range(2):
-        remote(
-            t_ref.at[image], tea.at[c], t_send, t_recv, across(2 * z + image)
-        ).start()
-
     band = ring // cq
     wcols = pl.ds(al(lax.rem(ring, cq) * cw, 128), cw)
     own_w = w_ref.at[band, :, wcols]
@@ -101,30 +110,95 @@
     sources = (k_ref, q_ref, v_ref)
     places = (kh.at[mine], qh.at[mine], va.at[mine, pl.ds(0, HD)])
 
-    def send_inputs(image):
+    def scatter_inputs(image):
         for a in range(3):
+            @pl.loop(1, nr)
+            def _(step):
+                head = lax.rem(ring + step, nr)
+                remote(
+                    sources[a].at[image, :, pl.ds(al(head * HD, HD), HD)], stage.at[image, a, ring],
+                    st_send.at[image, a], st_recv.at[image, a], in_plane(head),
+                ).start()
+
+            pltpu.make_async_copy(
+                sources[a].at[image, :, pl.ds(al(ring * HD, HD), HD)], stage.at[image, a, ring],
+                st_recv.at[image, a],
+            ).start()
+
+    def pass_inputs(image):
+        for a in range(3):
+            waiting(stage.at[image, a], st_recv.at[image, a])
+
             @pl.loop(1, nz)
             def _(step):
-                there = lax.rem(z + step, nz)
-                cols = pl.ds(al(there * HD, HD), HD)
+                plane = lax.rem(z + step, nz)
                 remote(
-                    sources[a].at[image, :, cols], places[a], in_send.at[a], in_recv.at[a],
-                    on_ring(2 * there + image),
+                    stage.at[image, a, plane], places[a], in_send.at[a], in_recv.at[a],
+                    on_ring(2 * plane + image),
                 ).start()
 
-            own = sources[a].at[image, :, pl.ds(al(z * HD, HD), HD)]
-
             @pl.when(c == image)
             def _():
-                pltpu.make_async_copy(own, places[a], in_recv.at[a]).start()
+                pltpu.make_async_copy(stage.at[image, a, z], places[a], in_recv.at[a]).start()
 
             @pl.when(c != image)
             def _():
                 remote(
-                    own, places[a], in_send.at[a], in_recv.at[a], on_ring(2 * z + image)
+                    stage.at[image, a, z], places[a], in_send.at[a], in_recv.at[a], on_ring(2 * z + image)
                 ).start()
 
-    send_inputs(0)
+    t_rows = SEG // tq
+    t_cols = enc // tc
+
+    def part_of(p):
+        rest = lax.rem(p, tq * tc)
+        return (
+            p // (tq * tc),
+            pl.ds(al(rest // tc * t_rows, t_rows), t_rows),
+            pl.ds(al(lax.rem(rest, tc) * t_cols, 128), t_cols),
+        )
+
+    def scatter_teacher():
+        @pl.loop(1, nr)
+        def _(step):
+            by = lax.rem(ring + step, nr)
+            image, rows_at, cols_at = part_of(by)
+            remote(
+                t_ref.at[image, rows_at, cols_at], t_stage.at[ring], t_send.at[0], t_recv.at[0], in_plane(by)
+            ).start()
+
+        image, rows_at, cols_at = part_of(ring)
+        pltpu.make_async_copy(t_ref.at[image, rows_at, cols_at], t_stage.at[ring], t_recv.at[0]).start()
+
+    t_image, t_rows_at, t_cols_at = part_of(ring)
+
+    def pass_teacher():
+        waiting(t_stage, t_recv.at[0])
+
+        @pl.loop(0, nr)
+        def _(step):
+            origin = lax.rem(z + nr // 2 + step, nr)
+            plane = lax.rem(origin + nr // 2, nr)
+            src = t_stage.at[origin]
+            dst = tea.at[c, t_rows_at, t_cols_at]
+            here = (ring == z) & (plane == z) & (t_image == c)
+
+            @pl.when(here)
+            def _():
+                pltpu.make_async_copy(src, dst, t_recv.at[1]).start()
+
+            @pl.when(jnp.logical_not(here))
+            def _():
+                remote(src, dst, t_send.at[1], t_recv.at[1], at(z, 2 * plane + t_image)).start()
+
+    scatter_inputs(0)
+    scatter_teacher()
+    scatter_inputs(1)
+    pass_inputs(0)
+
+    @pl.when(t_image == 0)
+    def _():
+        pass_teacher()
 
     part_w = wf.at[:, c, band, :, wcols]
     waiting(part_w, w_recv.at[0])
@@ -135,8 +209,15 @@
             part_w, part_w, w_send.at[1], w_recv.at[1], in_plane(lax.rem(ring + step, nr))
         ).start()
 
-    send_inputs(1)
-
+    pass_inputs(1)
+
+    @pl.when(t_image == 1)
+    def _():
+        pass_teacher()
+
+    length = len_ref[2 * z + c]
+    keys_at = lax.broadcasted_iota(jnp.int32, (1, total), 1)
+    kb_ref[...] = jnp.where(keys_at < length, 0.0, -1e30).astype(F32)
     va[:, HD:] = jnp.ones((total, HD), BF)
     acc_k[...] = jnp.zeros_like(acc_k)
     acc_v[...] = jnp.zeros_like(acc_v)
@@ -150,18 +231,11 @@
     def _():
         swap_w()
 
-    waiting(tea, t_recv)
-    for seg in range(2):
-        data = tea[seg].astype(F32)
-        center = data - jnp.mean(data, axis=-1, keepdims=True)
-        spread = jnp.mean(center * center, axis=-1, keepdims=True)
-        tea[seg] = (center * lax.rsqrt(spread + EPS) * gain_ref[...] + bias_ref[...]).astype(BF)
-
     waiting(kh, in_recv.at[0])
     waiting(qh, in_recv.at[1])
     waiting(va.at[:, pl.ds(0, HD)], in_recv.at[2])
 
-    first = z // per
+    first = ring // per
 
     @pl.loop(0, nb)
     def _(step):
@@ -181,22 +255,29 @@
         for part in range(per):
             there = block * per + part
             src = att_h.at[pl.ds(al(there * TOK, TOK), TOK)]
-            dst = rows.at[:, pl.ds(al(z * HD, HD), HD)]
-
-            @pl.when(there == z)
+            dst = rows.at[:, pl.ds(al(ring * HD, HD), HD)]
+
+            @pl.when(there == ring)
             def _():
                 pltpu.make_async_copy(src, dst, mid_recv.at[0]).start()
 
-            @pl.when(there != z)
-            def _():
-                remote(src, dst, mid_send.at[0], mid_recv.at[0], on_ring(2 * there + c)).start()
+            @pl.when(there != ring)
+            def _():
+                remote(src, dst, mid_send.at[0], mid_recv.at[0], in_plane(there)).start()
 
     @pl.when(c == 0)
     def _():
         swap_w()
 
+    waiting(tea, t_recv.at[1])
+    for seg in range(2):
+        data = tea[seg].astype(F32)
+        center = data - jnp.mean(data, axis=-1, keepdims=True)
+        spread = jnp.mean(center * center, axis=-1, keepdims=True)
+        tea[seg] = (center * lax.rsqrt(spread + EPS) * gain_ref[...][None, :] + bias_ref[...][None, :]).astype(BF)
+
+    waiting(rows, mid_recv.at[0])
     waiting(wf.at[:, 1 - c], w_recv.at[2])
-    waiting(rows, mid_recv.at[0])
 
     pieces = enc // 384
     inner = jnp.zeros((TOK, 1), F32)
@@ -216,7 +297,8 @@
     other = other / enc + EPS
     inverse = lax.rsqrt(own * other)
     cosine = inner * inverse
-    kept = keep_ref[...] * (-COEF / enc)
+    token = ring * TOK + lax.broadcasted_iota(jnp.int32, (TOK, 1), 0)
+    kept = jnp.where(token < length, -COEF / enc, 0.0).astype(F32)
     left = kept * inverse
     right = kept * (cosine / own)
     for piece in range(pieces):
@@ -226,38 +308,40 @@
 
     @pl.loop(0, nz // 2)
     def _(step):
-        pair = lax.rem(z // 2 + step, nz // 2)
+        pair = lax.rem(ring // 2 + step, nz // 2)
         weights = wf[pl.ds(pair * 2, 2)].reshape(2 * HD, enc)
         back = lax.dot_general(gal[...], weights, NT, preferred_element_type=F32).astype(BF)
         for part in range(2):
             there = pair * 2 + part
             gsend[there] = back[:, part * HD:(part + 1) * HD]
             src = gsend.at[there]
-            dst = gh.at[pl.ds(al(z * TOK, TOK), TOK)]
-
-            @pl.when(there == z)
+            dst = gh.at[pl.ds(al(ring * TOK, TOK), TOK)]
+
+            @pl.when(there == ring)
             def _():
                 pltpu.make_async_copy(src, dst, mid_recv.at[1]).start()
 
-            @pl.when(there != z)
-            def _():
-                remote(src, dst, mid_send.at[1], mid_recv.at[1], on_ring(2 * there + c)).start()
+            @pl.when(there != ring)
+            def _():
+                remote(src, dst, mid_send.at[1], mid_recv.at[1], in_plane(there)).start()
 
     waiting(gh, mid_recv.at[1])
 
-    my_cols = pl.ds(al(z * HD, HD), HD)
+    my_cols = pl.ds(al(ring * HD, HD), HD)
 
     def send_out(src_ref, out_ref, a, s):
         src = src_ref.at[pl.ds(al(s * SEG, SEG), SEG)]
         dst = out_ref.at[c, :, my_cols]
 
-        @pl.when(s == me)
+        here = (s == me) & (ring == z)
+
+        @pl.when(here)
         def _():
             pltpu.make_async_copy(src, dst, out_recv.at[a]).start()
 
-        @pl.when(s != me)
+        @pl.when(jnp.logical_not(here))
         def _():
-            remote(src, dst, out_send.at[a], out_recv.at[a], on_ring(s)).start()
+            remote(src, dst, out_send.at[a], out_recv.at[a], at(z, s)).start()
 
     segs = bq // SEG
 
@@ -290,17 +374,38 @@
     def _(step):
         send_out(gk_h, ok_ref, 1, lax.rem(me + step, ns))
 
-    waiting(tea, t_send)
     waiting(wf.at[pl.ds(0, nz - 1), c, band, :, wcols], w_send.at[0])
     waiting(wf.at[pl.ds(0, nr - 1), c], w_send.at[1])
     waiting(wf.at[:, c], w_send.at[2])
+    others = pl.ds(0, nr - 1)
+    waiting(t_stage.at[others], t_send.at[0])
+    t_here = (ring == z) & (t_image == c)
+
+    @pl.when(t_here)
+    def _():
+        waiting(t_stage.at[others], t_send.at[1])
+
+    @pl.when(jnp.logical_not(t_here))
+    def _():
+        waiting(t_stage, t_send.at[1])
+
+    for image in range(2):
+        for a in range(3):
+            waiting(stage.at[image, a, others], st_send.at[image, a])
     most = pl.ds(0, total - SEG)
     for a, buf in enumerate((kh.at[most], qh.at[most], va.at[most, pl.ds(0, HD)])):
         waiting(buf, in_send.at[a])
     waiting(att_h.at[pl.ds(0, total - TOK)], mid_send.at[0])
-    waiting(gsend.at[pl.ds(0, nz - 1)], mid_send.at[1])
+    waiting(gsend.at[others], mid_send.at[1])
     for a, buf in enumerate((gq_h, gk_h, gv_h)):
-        waiting(buf.at[most], out_send.at[a])
+        @pl.when(ring == z)
+        def _():
+            waiting(buf.at[most], out_send.at[a])
+
+        @pl.when(ring != z)
+        def _():
+            waiting(buf, out_send.at[a])
+
     for a, buf in enumerate((oq_ref, ok_ref, ov_ref)):
         waiting(buf, out_recv.at[a])
 
@@ -314,12 +419,8 @@
     enc = teacher.shape[-1]
     total = ns * seg
     bq = min(256, total // 2)
-    me = lax.axis_index("seq")
-    image = (lax.axis_index("grp") * ndp + lax.axis_index("dp")) * count + lax.rem(me, 2)
-    length = lax.dynamic_slice_in_dim(valid_len, image, 1)
-    key_bias = jnp.where(lax.iota(jnp.int32, total) < length, 0.0, -1e30).astype(F32)[None, :]
-    token = (me // 2) * TOK + lax.iota(jnp.int32, TOK)
-    keep = (token < length).astype(F32)[:, None]
+    tq = min(4, nr // 2)
+    tc = nr // (2 * tq)
     vm = pl.BlockSpec(memory_space=pltpu.VMEM)
     hbm = pl.BlockSpec(memory_space=pl.ANY)
     dma = pltpu.SemaphoreType.DMA
@@ -329,9 +430,12 @@
     return pl.pallas_call(
         functools.partial(kernel, nz, nr, ndp, bq),
         out_shape=[out, out, out],
-        in_specs=[hbm, hbm, hbm, hbm, hbm, vm, vm, vm, vm],
+        in_specs=[hbm, hbm, hbm, hbm, hbm, vm, vm, pl.BlockSpec(memory_space=pltpu.SMEM)],
         out_specs=[hbm, hbm, hbm],
         scratch_shapes=[
+            pltpu.VMEM((2, 3, nr, seg, HD), BF),
+            pltpu.VMEM((nr, seg // tq, enc // tc), BF),
+            pltpu.VMEM((1, total), F32),
             head,
             head,
             pltpu.VMEM((total, 2 * HD), BF),
@@ -351,12 +455,14 @@
             pltpu.VMEM((TOK, enc), BF),
             pltpu.VMEM((HD, total), F32),
             pltpu.VMEM((HD, total), F32),
-            dma((3,)),
-            dma((3,)),
-            dma((3,)),
-            dma((3,)),
-            dma,
-            dma,
+            dma((2, 3)),
+            dma((2, 3)),
+            dma((3,)),
+            dma((3,)),
+            dma((3,)),
+            dma((3,)),
+            dma((2,)),
+            dma((2,)),
             dma((2,)),
             dma((2,)),
             dma((3,)),
@@ -371,10 +477,9 @@
         value_states,
         projector.reshape(4, seg // 4, enc),
         teacher,
-        enc_gain[None, :],
-        enc_bias[None, :],
-        key_bias,
-        keep,
+        enc_gain,
+        enc_bias,
+        valid_len,
     )
 
 

time: 223 us -> 202 us (0.906)
  the two profiles are of different devices: /device:TPU:31 before, /device:TPU:7 now
where the time goes in v2:
time: 202 us
  Pallas kernels  198 us (98%)
  local copies, waits for them, and re-layouts  3.97 us (2%)
    pallas_call x1, Pallas kernels, shards(): pl.pallas_call(functools.partial(kernel, nz, nr, ndp, bq), out_shape=[out...  198 us

profile of v2, /device:TPU:7, one launch (start us, length us, event | category | flops | bytes accessed | tf_op | source)
XLA Modules:
  0.0 202.2 jit_solution(1303432042436903945)
XLA Ops:
  0.6 197.6 %shard_map.103 = (bf16[2,64,2048]{2,1,0:T(8,128)(2,1)}, bf16[2,64,2048]{2,1,0:T(8,128)(2,1)}, bf16[2,64,2048]{2,1,0:T(8,128)(2,1)}) custom-call(bf16[2,64,2048]{2,1,0:T(8,128)(2,1)} %q_ref.1, bf16[2,64,2048]{2,1,0:T(8,128)(2,1)} %k_ref.1, bf16[2,64,2048]{2,1,0:T(8,128)(2,1)} %v_ref.1, bf16[4,16,1536]{2,1,0:T(8,128)(2,1)} %bitcast.1, ...), custom_call_target="tpu_custom_call" | custom-call | tf_op jit(solution)/shard_map/pallas_call | solution.py:430
  198.3 0.0 copy-start.1
  198.3 1.9 copy.14
  200.2 0.0 copy-done.1
  200.2 0.0 copy-start
  200.2 0.8 copy.15
  201.0 0.4 copy-done
  201.4 0.8 copy.16
Async XLA Ops:
  198.3 2.0 copy-start.1
  200.2 1.2 copy-start

commit v3 on v2

--- a/solution.py
+++ b/solution.py
@@ -28,7 +28,7 @@
     q_ref, k_ref, v_ref, w_ref, t_ref, gain_ref, bias_ref, len_ref,
     oq_ref, ok_ref, ov_ref,
     stage, t_stage, kb_ref, qh, kh, va, wf, tea, att_h, rows, gsend, gh, gq_h, gk_h, gv_h,
-    expo, att_f, linv, aligned, gal, acc_k, acc_v,
+    expo, att_f, linv, aligned, gal, acc_q, grad_t, q_t, delta,
     st_send, st_recv, in_send, in_recv, w_send, w_recv, t_send, t_recv, mid_send, mid_recv, out_send, out_recv,
 ):
     ns = 2 * nz
@@ -97,14 +97,21 @@
     wcols = pl.ds(al(lax.rem(ring, cq) * cw, 128), cw)
     own_w = w_ref.at[band, :, wcols]
 
-    @pl.loop(1, nz)
-    def _(step):
-        there = lax.rem(z + step, nz)
-        remote(
-            own_w, wf.at[z, c, band, :, wcols], w_send.at[0], w_recv.at[0], on_ring(2 * there + c)
-        ).start()
-
-    pltpu.make_async_copy(own_w, wf.at[z, c, band, :, wcols], w_recv.at[0]).start()
+    own_place = wf.at[z // 4, lax.rem(z, 4), c, band, :, wcols]
+
+    @pl.loop(1, nz // 4)
+    def _(step):
+        there = lax.rem(z + 4 * step, nz)
+        remote(own_w, own_place, w_send.at[0], w_recv.at[0], on_ring(2 * there + c)).start()
+
+    pltpu.make_async_copy(own_w, own_place, w_recv.at[0]).start()
+
+    def pass_w():
+        class_w = wf.at[:, lax.rem(z, 4), c, band, :, wcols]
+        waiting(class_w, w_recv.at[0])
+        for apart in (1, nz - 1, 2):
+            there = lax.rem(z + apart, nz)
+            remote(class_w, class_w, w_send.at[3], w_recv.at[3], on_ring(2 * there + c)).start()
 
     mine = pl.ds(al(me * SEG, SEG), SEG)
     sources = (k_ref, q_ref, v_ref)
@@ -194,14 +201,15 @@
     scatter_inputs(0)
     scatter_teacher()
     scatter_inputs(1)
+    pass_w()
     pass_inputs(0)
 
     @pl.when(t_image == 0)
     def _():
         pass_teacher()
 
-    part_w = wf.at[:, c, band, :, wcols]
-    waiting(part_w, w_recv.at[0])
+    part_w = wf.at[:, :, c, band, :, wcols]
+    waiting(wf.at[:, pl.ds(0, 3), c, band, :, wcols], w_recv.at[3])
 
     @pl.loop(1, nr)
     def _(step):
@@ -219,12 +227,13 @@
     keys_at = lax.broadcasted_iota(jnp.int32, (1, total), 1)
     kb_ref[...] = jnp.where(keys_at < length, 0.0, -1e30).astype(F32)
     va[:, HD:] = jnp.ones((total, HD), BF)
-    acc_k[...] = jnp.zeros_like(acc_k)
-    acc_v[...] = jnp.zeros_like(acc_v)
+    acc_q[...] = jnp.zeros_like(acc_q)
+
+    most_w = expo.at[pl.ds(0, (nr - 1) * nz * (SEG // 4) * cw // total)]
 
     def swap_w():
-        waiting(wf.at[pl.ds(0, nr - 1), c], w_recv.at[1])
-        half = wf.at[:, c]
+        waiting(most_w, w_recv.at[1])
+        half = wf.at[:, :, c]
         remote(half, half, w_send.at[2], w_recv.at[2], on_ring(2 * z + 1 - c)).start()
 
     @pl.when(c == 1)
@@ -277,7 +286,7 @@
         tea[seg] = (center * lax.rsqrt(spread + EPS) * gain_ref[...][None, :] + bias_ref[...][None, :]).astype(BF)
 
     waiting(rows, mid_recv.at[0])
-    waiting(wf.at[:, 1 - c], w_recv.at[2])
+    waiting(wf.at[:, :, 1 - c], w_recv.at[2])
 
     pieces = enc // 384
     inner = jnp.zeros((TOK, 1), F32)
@@ -285,7 +294,7 @@
     other = jnp.zeros((TOK, 1), F32)
     for piece in range(pieces):
         cols = slice(piece * 384, (piece + 1) * 384)
-        weights = wf[:, :, :, :, cols].reshape(nz * HD, 384)
+        weights = wf[:, :, :, :, :, cols].reshape(nz * HD, 384)
         out = jnp.dot(rows[...], weights, preferred_element_type=F32)
         aligned[:, cols] = out
         tgt = tea[:, :, cols].reshape(TOK, 384).astype(F32)
@@ -309,7 +318,7 @@
     @pl.loop(0, nz // 2)
     def _(step):
         pair = lax.rem(ring // 2 + step, nz // 2)
-        weights = wf[pl.ds(pair * 2, 2)].reshape(2 * HD, enc)
+        weights = wf[pair // 2, pl.ds(lax.rem(pair, 2) * 2, 2)].reshape(2 * HD, enc)
         back = lax.dot_general(gal[...], weights, NT, preferred_element_type=F32).astype(BF)
         for part in range(2):
             there = pair * 2 + part
@@ -346,37 +355,43 @@
     segs = bq // SEG
 
     @pl.loop(0, nb)
-    def _(step):
-        block = lax.rem(first + step, nb)
+    def _(block):
         span = pl.ds(al(block * bq, bq), bq)
         grad = gh[span].astype(F32) * linv[span]
         grad_b = grad.astype(BF)
-        delta = jnp.sum(grad_b.astype(F32) * att_f[span], axis=-1, keepdims=True)
-        raised = expo[span]
-        grad_p = lax.dot_general(grad_b, va[:, :HD], NT, preferred_element_type=F32)
-        grad_s = (raised.astype(F32) * (grad_p - delta)).astype(BF)
-        acc_v[...] += jnp.dot(grad.T.astype(BF), raised, preferred_element_type=F32)
-        acc_k[...] += jnp.dot(qh[span].astype(F32).T.astype(BF), grad_s, preferred_element_type=F32)
-        grad_q = jnp.dot(grad_s, kh[...], preferred_element_type=F32)
-        gq_h[span] = (grad_q * scale).astype(BF)
+        gh[span] = grad_b
+        grad_t[:, span] = grad.T.astype(BF)
+        q_t[:, span] = qh[span].astype(F32).T.astype(BF)
+        delta[span] = jnp.sum(grad_b.astype(F32) * att_f[span], axis=-1, keepdims=True)
+
+    @pl.loop(0, nb)
+    def _(step):
+        block = lax.rem(z // per + step, nb)
+        span = pl.ds(al(block * bq, bq), bq)
+        raised = expo[:, span]
+        grad_v = jnp.dot(grad_t[...], raised, preferred_element_type=F32)
+        gv_h[span] = grad_v.T.astype(BF)
         for part in range(segs):
-            send_out(gq_h, oq_ref, 0, block * segs + part)
-
-    gv_h[...] = acc_v[...].T.astype(BF)
+            send_out(gv_h, ov_ref, 2, block * segs + part)
+        grad_p = lax.dot_general(gh[...], va[span, :HD], NT, preferred_element_type=F32)
+        grad_s = (raised.astype(F32) * (grad_p - delta[...])).astype(BF)
+        grad_k = jnp.dot(q_t[...], grad_s, preferred_element_type=F32)
+        gk_h[span] = (grad_k * scale).T.astype(BF)
+        for part in range(segs):
+            send_out(gk_h, ok_ref, 1, block * segs + part)
+        acc_q[...] += jnp.dot(grad_s, kh[span], preferred_element_type=F32)
+
+    gq_h[...] = (acc_q[...] * scale).astype(BF)
 
     @pl.loop(0, ns)
     def _(step):
-        send_out(gv_h, ov_ref, 2, lax.rem(me + step, ns))
-
-    gk_h[...] = (acc_k[...] * scale).T.astype(BF)
-
-    @pl.loop(0, ns)
-    def _(step):
-        send_out(gk_h, ok_ref, 1, lax.rem(me + step, ns))
-
-    waiting(wf.at[pl.ds(0, nz - 1), c, band, :, wcols], w_send.at[0])
-    waiting(wf.at[pl.ds(0, nr - 1), c], w_send.at[1])
-    waiting(wf.at[:, c], w_send.at[2])
+        send_out(gq_h, oq_ref, 0, lax.rem(me + step, ns))
+
+    if nz > 4:
+        waiting(wf.at[pl.ds(0, nz // 4 - 1), 0, c, band, :, wcols], w_send.at[0])
+    waiting(wf.at[:, pl.ds(0, 3), c, band, :, wcols], w_send.at[3])
+    waiting(most_w, w_send.at[1])
+    waiting(wf.at[:, :, c], w_send.at[2])
     others = pl.ds(0, nr - 1)
     waiting(t_stage.at[others], t_send.at[0])
     t_here = (ring == z) & (t_image == c)
@@ -439,7 +454,7 @@
             head,
             head,
             pltpu.VMEM((total, 2 * HD), BF),
-            pltpu.VMEM((nz, 2, 4, seg // 4, enc), BF),
+            pltpu.VMEM((nz // 4, 4, 2, 4, seg // 4, enc), BF),
             pltpu.VMEM((2, seg, enc), BF),
             head,
             pltpu.VMEM((TOK, width), BF),
@@ -453,14 +468,16 @@
             head_f,
             pltpu.VMEM((TOK, enc), F32),
             pltpu.VMEM((TOK, enc), BF),
-            pltpu.VMEM((HD, total), F32),
-            pltpu.VMEM((HD, total), F32),
+            head_f,
+            pltpu.VMEM((HD, total), BF),
+            pltpu.VMEM((HD, total), BF),
+            pltpu.VMEM((total, 1), F32),
             dma((2, 3)),
             dma((2, 3)),
             dma((3,)),
             dma((3,)),
-            dma((3,)),
-            dma((3,)),
+            dma((4,)),
+            dma((4,)),
             dma((2,)),
             dma((2,)),
             dma((2,)),

time: 202 us -> 208 us (1.030)
  the two profiles are of different devices: /device:TPU:7 before, /device:TPU:3 now
where the time goes in v3:
time: 208 us
  Pallas kernels  203 us (98%)
  local copies, waits for them, and re-layouts  3.97 us (2%)
    pallas_call x1, Pallas kernels, shards(): pl.pallas_call(functools.partial(kernel, nz, nr, ndp, bq), out_shape=[out...  203 us

profile of v3, /device:TPU:3, one launch (start us, length us, event | category | flops | bytes accessed | tf_op | source)
XLA Modules:
  0.0 207.8 jit_solution(3920489599873735743)
XLA Ops:
  0.6 203.2 %shard_map.103 = (bf16[2,64,2048]{2,1,0:T(8,128)(2,1)}, bf16[2,64,2048]{2,1,0:T(8,128)(2,1)}, bf16[2,64,2048]{2,1,0:T(8,128)(2,1)}) custom-call(bf16[2,64,2048]{2,1,0:T(8,128)(2,1)} %q_ref.1, bf16[2,64,2048]{2,1,0:T(8,128)(2,1)} %k_ref.1, bf16[2,64,2048]{2,1,0:T(8,128)(2,1)} %v_ref.1, bf16[4,16,1536]{2,1,0:T(8,128)(2,1)} %bitcast.1, ...), custom_call_target="tpu_custom_call" | custom-call | tf_op jit(solution)/shard_map/pallas_call | solution.py:445
  203.9 0.0 copy-start.1
  203.9 1.9 copy.14
  205.8 0.0 copy-done.1
  205.8 0.0 copy-start
  205.8 0.8 copy.15
  206.6 0.4 copy-done
  207.0 0.8 copy.16
Async XLA Ops:
  203.9 2.0 copy-start.1
  205.8 1.2 copy-start

commit v4 on v2

--- a/solution.py
+++ b/solution.py
@@ -34,8 +34,9 @@
     ns = 2 * nz
     total = ns * SEG
     enc = t_ref.shape[-1]
-    cq = nr // 4
-    cw = enc // cq
+    nx = ndp // 2
+    ny = nr // nx
+    cw = enc // ny
     nb = total // bq
     per = bq // TOK
     tq = min(4, nr // 2)
@@ -93,8 +94,10 @@
     def waiting(view, sem):
         pltpu.make_async_copy(view, view, sem).wait()
 
-    band = ring // cq
-    wcols = pl.ds(al(lax.rem(ring, cq) * cw, 128), cw)
+    x = lax.axis_index("dp") // 2
+    y = lax.axis_index("grp") * 2 + lax.rem(lax.axis_index("dp"), 2)
+    band = x
+    wcols = pl.ds(al(y * cw, 128), cw)
     own_w = w_ref.at[band, :, wcols]
 
     @pl.loop(1, nz)
@@ -200,20 +203,37 @@
     def _():
         pass_teacher()
 
-    part_w = wf.at[:, c, band, :, wcols]
-    waiting(part_w, w_recv.at[0])
-
-    @pl.loop(1, nr)
-    def _(step):
-        remote(
-            part_w, part_w, w_send.at[1], w_recv.at[1], in_plane(lax.rem(ring + step, nr))
-        ).start()
+    waiting(wf.at[:, c, band, :, wcols], w_recv.at[0])
+    front, rear = pl.ds(0, nz // 2), pl.ds(nz // 2, nz // 2)
+
+    def along_x(src, sem):
+        for step in range(1, nx):
+            there = {"dp": lax.rem(x + step, nx) * 2 + lax.rem(y, 2)}
+            remote(src, src, w_send.at[sem], w_recv.at[sem], there).start()
+
+    def along_y(src, sem):
+        for step in range(1, ny):
+            there = lax.rem(y + step, ny)
+            remote(
+                src, src, w_send.at[sem], w_recv.at[sem], {"grp": there // 2, "dp": x * 2 + lax.rem(there, 2)}
+            ).start()
+
+    most_y = pl.ds(0, (ny - 1) * cw)
+    most_x = pl.ds(0, max(nx - 1, 1))
+    along_x(wf.at[front, c, band, :, wcols], 1)
+    along_y(wf.at[rear, c, band, :, wcols], 3)
 
     pass_inputs(1)
 
     @pl.when(t_image == 1)
     def _():
         pass_teacher()
+
+    if nx > 1:
+        waiting(wf.at[front, c, most_x, :, wcols], w_recv.at[1])
+    along_y(wf.at[front, c, :, :, wcols], 4)
+    waiting(wf.at[rear, c, band, :, most_y], w_recv.at[3])
+    along_x(wf.at[rear, c, band], 5)
 
     length = len_ref[2 * z + c]
     keys_at = lax.broadcasted_iota(jnp.int32, (1, total), 1)
@@ -223,7 +243,9 @@
     acc_v[...] = jnp.zeros_like(acc_v)
 
     def swap_w():
-        waiting(wf.at[pl.ds(0, nr - 1), c], w_recv.at[1])
+        waiting(wf.at[front, c, :, :, most_y], w_recv.at[4])
+        if nx > 1:
+            waiting(wf.at[rear, c, most_x], w_recv.at[5])
         half = wf.at[:, c]
         remote(half, half, w_send.at[2], w_recv.at[2], on_ring(2 * z + 1 - c)).start()
 
@@ -375,7 +397,11 @@
         send_out(gk_h, ok_ref, 1, lax.rem(me + step, ns))
 
     waiting(wf.at[pl.ds(0, nz - 1), c, band, :, wcols], w_send.at[0])
-    waiting(wf.at[pl.ds(0, nr - 1), c], w_send.at[1])
+    if nx > 1:
+        waiting(wf.at[front, c, most_x, :, wcols], w_send.at[1])
+        waiting(wf.at[rear, c, most_x], w_send.at[5])
+    waiting(wf.at[rear, c, band, :, most_y], w_send.at[3])
+    waiting(wf.at[front, c, :, :, most_y], w_send.at[4])
     waiting(wf.at[:, c], w_send.at[2])
     others = pl.ds(0, nr - 1)
     waiting(t_stage.at[others], t_send.at[0])
@@ -439,7 +465,7 @@
             head,
             head,
             pltpu.VMEM((total, 2 * HD), BF),
-            pltpu.VMEM((nz, 2, 4, seg // 4, enc), BF),
+            pltpu.VMEM((nz, 2, ndp // 2, 2 * seg // ndp, enc), BF),
             pltpu.VMEM((2, seg, enc), BF),
             head,
             pltpu.VMEM((TOK, width), BF),
@@ -459,8 +485,8 @@
             dma((2, 3)),
             dma((3,)),
             dma((3,)),
-            dma((3,)),
-            dma((3,)),
+            dma((6,)),
+            dma((6,)),
             dma((2,)),
             dma((2,)),
             dma((2,)),
@@ -475,7 +501,7 @@
         queries,
         key_states,
         value_states,
-        projector.reshape(4, seg // 4, enc),
+        projector.reshape(ndp // 2, 2 * seg // ndp, enc),
         teacher,
         enc_gain,
         enc_bias,

time: 202 us -> 194 us (0.960)
  the two profiles are of different devices: /device:TPU:7 before, /device:TPU:5 now
where the time goes in v4:
time: 194 us
  Pallas kernels  189 us (97%)
  local copies, waits for them, and re-layouts  3.97 us (2%)
    pallas_call x1, Pallas kernels, shards(): pl.pallas_call(functools.partial(kernel, nz, nr, ndp, bq), out_shape=[out...  189 us
    unnamed x7, local copies, waits for them, and re-layouts  3.97 us

profile of v4, /device:TPU:5, one launch (start us, length us, event | category | flops | bytes accessed | tf_op | source)
XLA Modules:
  0.0 194.1 jit_solution(2189232236668622790)
XLA Ops:
  0.6 189.5 %shard_map.103 = (bf16[2,64,2048]{2,1,0:T(8,128)(2,1)}, bf16[2,64,2048]{2,1,0:T(8,128)(2,1)}, bf16[2,64,2048]{2,1,0:T(8,128)(2,1)}) custom-call(bf16[2,64,2048]{2,1,0:T(8,128)(2,1)} %q_ref.1, bf16[2,64,2048]{2,1,0:T(8,128)(2,1)} %k_ref.1, bf16[2,64,2048]{2,1,0:T(8,128)(2,1)} %v_ref.1, bf16[4,16,1536]{2,1,0:T(8,128)(2,1)} %bitcast.1, ...), custom_call_target="tpu_custom_call" | custom-call | tf_op jit(solution)/shard_map/pallas_call | solution.py:456
  190.1 0.0 copy-start.1
  190.1 1.9 copy.14
  192.0 0.0 copy-done.1
  192.0 0.0 copy-start
  192.1 0.8 copy.15
  192.8 0.4 copy-done
  193.3 0.8 copy.16
Async XLA Ops:
  190.1 2.0 %copy-start.1 = (bf16[2,64,2048]{2,1,0:T(8,128)(2,1)S(1)}, bf16[2,64,2048]{2,1,0:T(8,128)(2,1)}, u32[]{:S(2)}) copy-start(bf16[2,64,2048]{2,1,0:T(8,128)(2,1)} %get-tuple-element.7) | copy-start | bytes 1572868
  192.0 1.2 copy-start

commit v5 on v4

--- a/solution.py
+++ b/solution.py
@@ -225,15 +225,15 @@
 
     pass_inputs(1)
 
-    @pl.when(t_image == 1)
-    def _():
-        pass_teacher()
-
     if nx > 1:
         waiting(wf.at[front, c, most_x, :, wcols], w_recv.at[1])
     along_y(wf.at[front, c, :, :, wcols], 4)
     waiting(wf.at[rear, c, band, :, most_y], w_recv.at[3])
     along_x(wf.at[rear, c, band], 5)
+
+    @pl.when(t_image == 1)
+    def _():
+        pass_teacher()
 
     length = len_ref[2 * z + c]
     keys_at = lax.broadcasted_iota(jnp.int32, (1, total), 1)

time: 194 us -> 194 us (level)
  no operation moved by 1% of the time
where the time goes in v5:
time: 194 us
  Pallas kernels  189 us (97%)
  local copies, waits for them, and re-layouts  3.97 us (2%)
    pallas_call x1, Pallas kernels, shards(): pl.pallas_call(functools.partial(kernel, nz, nr, ndp, bq), out_shape=[out...  189 us
    unnamed x7, local copies, waits for them, and re-layouts  3.97 us

profile of v5, /device:TPU:5, one launch (start us, length us, event | category | flops | bytes accessed | tf_op | source)
XLA Modules:
  0.0 194.1 jit_solution(16374224139777694506)
XLA Ops:
  0.6 189.5 %shard_map.103 = (bf16[2,64,2048]{2,1,0:T(8,128)(2,1)}, bf16[2,64,2048]{2,1,0:T(8,128)(2,1)}, bf16[2,64,2048]{2,1,0:T(8,128)(2,1)}) custom-call(bf16[2,64,2048]{2,1,0:T(8,128)(2,1)} %q_ref.1, bf16[2,64,2048]{2,1,0:T(8,128)(2,1)} %k_ref.1, bf16[2,64,2048]{2,1,0:T(8,128)(2,1)} %v_ref.1, bf16[4,16,1536]{2,1,0:T(8,128)(2,1)} %bitcast.1, ...), custom_call_target="tpu_custom_call" | custom-call | tf_op jit(solution)/shard_map/pallas_call | solution.py:456
  190.1 0.0 copy-start.1
  190.1 1.9 copy.14
  192.0 0.0 copy-done.1
  192.0 0.0 copy-start
  192.1 0.8 copy.15
  192.8 0.4 copy-done
  193.3 0.8 copy.16
Async XLA Ops:
  190.1 2.0 %copy-start.1 = (bf16[2,64,2048]{2,1,0:T(8,128)(2,1)S(1)}, bf16[2,64,2048]{2,1,0:T(8,128)(2,1)}, u32[]{:S(2)}) copy-start(bf16[2,64,2048]{2,1,0:T(8,128)(2,1)} %get-tuple-element.7) | copy-start | bytes 1572868
  192.0 1.2 copy-start
